TPU v7x, 256 devices: a whole 4x4x8 slice. The times are simulated.
256 devices in a mesh: pw: 32 (over z_lo, y, core), band: 8 (over x, z_hi).
Axes of the slice: x: 4, y: 4, z: 8 (z_hi: 2, z_lo: 4; z = z_hi * 4 + z_lo), core: 2. Of those that a mesh axis runs over, the one named last changes fastest.
Arguments:
- waves: bfloat16 [2, 40960, 7168], P(None, 'pw', 'band'), may hold values from -6 to 6
- projectors: bfloat16 [2, 128, 40960], P(None, 'band', 'pw'), may hold values from -0.01953125 to 0.01953125
- coupling: float32 [12, 13, 13], replicated, may hold values from -32.19938 to 32.19938
- offsets: int32 [12], replicated, may hold values from 0 to 119, as said below
- counts: int32 [12], replicated, may hold values from 9 to 13, as said below
Outputs:
- applied: bfloat16 [2, 40960, 7168], P(None, 'pw', 'band')
Inputs may be any that keep to these rules, and one draw needn't show every extreme that they name: `counts`: each atom has 9 or 13 projectors, exactly 5 atoms have 13, so the atoms fill all 128 projectors. offsets are the running sums of counts before each atom, so atoms take consecutive projectors in order.
All inputs are finite; a program needn't handle non-finite values.
Results may differ from a plain program's by a relative error of at most 0.0049.
Values may be sent and summed in bfloat16 or wider, within the bound.
No kernel may reach another device: no remote copies, remote signals or barrier semaphores. Data moves between devices by JAX's collectives and lax.ppermute only.
A program may use at most 64 MiB of HBM per device.

v0:
```python
import jax
import jax.numpy as jnp
from jax import lax
from jax.sharding import PartitionSpec as P

NP = 128
M = 13


def coupling_block(coupling, offsets, counts):
    proj = jnp.arange(NP, dtype=jnp.int32)
    local = jnp.arange(M, dtype=jnp.int32)
    target = offsets[:, None] + local[None, :]
    select = (proj[None, :, None] == target[:, None, :]) & (
        local[None, None, :] < counts[:, None, None]
    )
    select = select.astype(jnp.float32)
    sym = (coupling + jnp.swapaxes(coupling, 1, 2)) * 0.5
    return jnp.einsum("api,aij,aqj->pq", select, sym, select, precision=lax.Precision.HIGHEST)


def project(rows, waves):
    real = jnp.dot(rows[0], waves[0], preferred_element_type=jnp.float32) + jnp.dot(
        rows[1], waves[1], preferred_element_type=jnp.float32
    )
    imag = jnp.dot(rows[0], waves[1], preferred_element_type=jnp.float32) - jnp.dot(
        rows[1], waves[0], preferred_element_type=jnp.float32
    )
    return jnp.stack([real, imag])


def spread_back(rows, coupled):
    dims = (((0,), (0,)), ((), ()))
    real = lax.dot_general(
        rows[0], coupled[0], dims, preferred_element_type=jnp.float32
    ) - lax.dot_general(rows[1], coupled[1], dims, preferred_element_type=jnp.float32)
    imag = lax.dot_general(
        rows[0], coupled[1], dims, preferred_element_type=jnp.float32
    ) + lax.dot_general(rows[1], coupled[0], dims, preferred_element_type=jnp.float32)
    return jnp.stack([real, imag])


def shards(waves, projectors, coupling, offsets, counts):
    block = coupling_block(coupling, offsets, counts)
    gathered = lax.all_gather(projectors, "band", axis=1, tiled=True)
    partial_coeffs = project(gathered, waves)
    coeffs = lax.psum(partial_coeffs, "pw")
    coupled = jnp.einsum("pq,kqb->kpb", block, coeffs, precision=lax.Precision.HIGHEST).astype(
        jnp.bfloat16
    )
    result = spread_back(gathered, coupled)
    return result.astype(jnp.bfloat16)


def solution(mesh):
    placed = (P(None, "pw", "band"), P(None, "band", "pw"), P(), P(), P())
    return jax.shard_map(
        shards, mesh=mesh, in_specs=placed, out_specs=P(None, "pw", "band"), check_vma=False
    )
```

profile of v0, /device:TPU:2, one launch (start us, length us, event | category | flops | bytes accessed | tf_op | source)
XLA Modules:
  0.0 365.1 jit_solution(13705950301523723169)
XLA Ops:
  6.5 0.0 all-reduce.2.cloned.1.call-start
  6.5 0.0 copy-start.3
  6.5 54.1 %all_gather.3 = bf16[2,128,1280]{2,1,0:T(8,128)(2,1)S(1)} all-gather(bf16[2,16,1280]{2,1,0:T(8,128)(2,1)} %param.6), channel_id=1, replica_groups=mesh['pw'=32,'band'=8] {'band'}, dimensions={1}, use_global_device_ids=true | all-gather | bytes 737280 | tf_op jit(solution)/shard_map/all_gather | solution.py:45
  60.6 2.2 fusion.2
  62.8 2.2 fusion.4
  64.9 0.0 copy-done.3
  65.0 0.0 copy-start
  65.0 0.0 copy-start.1
  65.0 0.0 copy-start.2
  65.0 0.5 fusion.24
  65.5 0.5 fusion.18
  66.0 1.0 pad_maximum_fusion.1
  67.0 0.0 all-reduce.2.cloned.1.call-update
  67.0 0.0 copy-done
  67.1 0.2 copy.6
  67.2 0.0 copy-done.1
  67.2 0.1 iota_compare_fusion.1
  67.3 0.0 copy-done.2
  67.3 0.1 iota_add_fusion
  67.4 0.8 fusion.30
  68.1 0.8 fusion.28
  69.0 273.7 %all-reduce.2.cloned.1.call-done = f32[2,128,896]{2,1,0:T(8,128)} async-done(((f32[2,128,896]{2,1,0:T(8,128)}), f32[2,128,896]{2,1,0:T(8,128)}) %all-reduce.2.cloned.1.call-update) | async-done | bytes 917520 | tf_op jit(solution)/shard_map/psum | solution.py:47
  342.7 2.8 fusion.14
  345.5 0.7 fusion.36
  346.2 0.7 fusion.37
  347.0 0.8 fusion.1
  347.7 0.8 fusion
  348.5 2.5 pad_maximum_fusion
  350.9 7.3 %copy.8 = bf16[2,1280,896]{2,1,0:T(8,128)(2,1)} copy(bf16[2,1280,896]{1,2,0:T(8,128)(2,1)} %pad_maximum_fusion) | data formatting | bytes 9175040 | tf_op jit(solution)/shard_map/stack | solution.py:40
Async XLA Ops:
  6.5 336.2 %all-reduce.2.cloned.1.call-start = ((), (), s32[]{:S(2)}) async-start(), calls=%async_computation | async-start | bytes 1835008 | tf_op jit(solution)/shard_map/psum | solution.py:47
  6.5 58.4 %copy-start.3 = (bf16[2,1280,896]{2,1,0:T(8,128)(2,1)S(1)}, bf16[2,1280,896]{2,1,0:T(8,128)(2,1)}, u32[]{:S(2)}) copy-start(bf16[2,1280,896]{2,1,0:T(8,128)(2,1)} %param.5) | copy-start | bytes 13762564
  65.0 2.1 copy-start
  65.0 2.2 copy-start.1
  65.0 2.3 copy-start.2
Sparse Core Ops, SparseCore 0:
  67.2 275.4 all-reduce.1
where the time goes:
time: 365 us
  waiting for transfers between devices  274 us (75%)
  blocking collectives  54.1 us (15%)
  between operations  13.5 us (4%)
  matrix products  12.7 us (3%)
  local copies, waits for them, and re-layouts  7.46 us (2%)
    psum x1, waiting for transfers between devices, shards(): coeffs = lax.psum(partial_coeffs, 'pw')  274 us
    all_gather x1, blocking collectives, shards(): gathered = lax.all_gather(projectors, 'band', axis=1, tiled=True)  54.1 us
  transfers between devices with their start and end apart: 1, of which 1 were waited for; matrix products, arithmetic and copies ran while one was open for 1% of the time, Pallas kernels for 0%

commit v1 on v0

--- a/solution.py
+++ b/solution.py
@@ -5,6 +5,11 @@
 
 NP = 128
 M = 13
+
+
+def gather_and_add(x, axis):
+    parts = lax.all_gather(x, axis)
+    return jnp.sum(parts, axis=0)
 
 
 def coupling_block(coupling, offsets, counts):
@@ -44,7 +49,7 @@
     block = coupling_block(coupling, offsets, counts)
     gathered = lax.all_gather(projectors, "band", axis=1, tiled=True)
     partial_coeffs = project(gathered, waves)
-    coeffs = lax.psum(partial_coeffs, "pw")
+    coeffs = gather_and_add(partial_coeffs, "pw")
     coupled = jnp.einsum("pq,kqb->kpb", block, coeffs, precision=lax.Precision.HIGHEST).astype(
         jnp.bfloat16
     )

time: 365 us -> 266 us (0.73)
  waiting for transfers between devices: 274 us -> 164 us
  other arithmetic: 3.59 us -> 14.1 us
    psum x1 -> x0, waiting for transfers between devices: 274 us -> none  [shards(): coeffs = lax.psum(partial_coeffs, 'pw')]
    all_gather x0 -> x1, waiting for transfers between devices: none -> 164 us  [gather_and_add(): parts = lax.all_gather(x, axis)]
    reduce_sum x0 -> x1, other arithmetic: none -> 10.5 us  [gather_and_add(): return jnp.sum(parts, axis=0)]
where the time goes in v1:
time: 266 us; the launch traced here: 265 us
  waiting for transfers between devices  164 us (62%)
  blocking collectives  54.1 us (20%)
  other arithmetic  14.1 us (5%)
  between operations  13.5 us (5%)
  matrix products  11.5 us (4%)
  local copies, waits for them, and re-layouts  7.46 us (3%)
    all_gather x1, waiting for transfers between devices, gather_and_add(): parts = lax.all_gather(x, axis)  164 us
    all_gather x1, blocking collectives, shards(): gathered = lax.all_gather(projectors, 'band', axis=1, tiled=True)  54.1 us
    reduce_sum x1, other arithmetic, gather_and_add(): return jnp.sum(parts, axis=0)  10.5 us
    another operation x1, local copies, waits for them, and re-layouts, spread_back(): return jnp.stack([real, imag])  7.27 us
  transfers between devices with their start and end apart: 1, of which 1 were waited for; matrix products, arithmetic and copies ran while one was open for 1% of the time, Pallas kernels for 0%

profile of v1, /device:TPU:2, one launch (start us, length us, event | category | flops | bytes accessed | tf_op | source)
XLA Modules:
  0.0 264.8 jit_solution(17942068290631853248)
XLA Ops:
  6.5 0.0 all-gather.3.cloned.1.call-start
  6.5 0.0 copy-start.3
  6.5 54.1 %all_gather.9 = bf16[2,128,1280]{2,1,0:T(8,128)(2,1)S(1)} all-gather(bf16[2,16,1280]{2,1,0:T(8,128)(2,1)} %param.6), channel_id=1, replica_groups=mesh['pw'=32,'band'=8] {'band'}, dimensions={1}, use_global_device_ids=true | all-gather | bytes 737280 | tf_op jit(solution)/shard_map/all_gather | solution.py:50
  60.6 2.2 fusion.4
  62.8 2.2 fusion.2
  64.9 0.0 copy-done.3
  65.0 0.0 copy-start
  65.0 0.0 copy-start.1
  65.0 0.0 copy-start.2
  65.0 0.5 fusion.18
  65.5 0.5 fusion.24
  66.0 1.0 pad_maximum_fusion.1
  67.0 0.0 all-gather.3.cloned.1.call-update
  67.0 0.0 copy-done
  67.1 0.2 copy.8
  67.2 0.0 copy-done.1
  67.2 0.1 iota_compare_fusion.1
  67.3 0.0 copy-done.2
  67.3 0.1 iota_add_fusion
  67.4 0.8 fusion.30
  68.1 0.8 fusion.28
  69.0 164.2 %all-gather.3.cloned.1.call-done = f32[64,128,896]{2,1,0:T(8,128)} async-done(((f32[2,128,896]{2,1,0:T(8,128)}), f32[64,128,896]{2,1,0:T(8,128)}) %all-gather.3.cloned.1.call-update) | async-done | bytes 29360144 | tf_op jit(solution)/shard_map/all_gather | solution.py:11
  233.1 10.5 %reduce_sum.9 = f32[2,128,896]{2,1,0:T(8,128)S(1)} reduce(f32[32,2,128,896]{3,2,1,0:T(8,128)} %bitcast.62, f32[]{:T(128)} %constant.0.clone.1), dimensions={0}, to_apply=%region_0.0 | reduce | flops 7110656 | bytes 30277636 | tf_op jit(solution)/shard_map/reduce_sum | solution.py:12
  243.6 1.6 fusion.14
  245.2 0.7 fusion.37
  246.0 0.7 fusion.36
  246.7 0.8 fusion
  247.5 0.8 fusion.1
  248.2 2.5 pad_maximum_fusion
  250.7 7.3 %copy.10 = bf16[2,1280,896]{2,1,0:T(8,128)(2,1)} copy(bf16[2,1280,896]{1,2,0:T(8,128)(2,1)} %pad_maximum_fusion) | data formatting | bytes 9175040 | tf_op jit(solution)/shard_map/stack | solution.py:45
Async XLA Ops:
  6.5 226.6 %all-gather.3.cloned.1.call-start = ((), (), s32[]{:S(2)}) async-start(), calls=%async_computation | async-start | bytes 30277632 | tf_op jit(solution)/shard_map/all_gather | solution.py:11
  6.5 58.4 %copy-start.3 = (bf16[2,1280,896]{2,1,0:T(8,128)(2,1)S(1)}, bf16[2,1280,896]{2,1,0:T(8,128)(2,1)}, u32[]{:S(2)}) copy-start(bf16[2,1280,896]{2,1,0:T(8,128)(2,1)} %param.5) | copy-start | bytes 13762564
  65.0 2.1 copy-start
  65.0 2.2 copy-start.1
  65.0 2.3 copy-start.2
Sparse Core Ops, SparseCore 0:
  67.2 165.9 all-gather.2

commit v2 on v0

--- a/solution.py
+++ b/solution.py
@@ -1,3 +1,4 @@
+import functools
 import jax
 import jax.numpy as jnp
 from jax import lax
@@ -5,6 +6,21 @@
 
 NP = 128
 M = 13
+
+
+def remake_slices_all(vals, mesh_name, dim_no):
+    return jnp.concatenate(
+        jax.lax.all_to_all(
+            jnp.stack([vals] * jax.lax.axis_size(mesh_name), axis=0),
+            mesh_name,
+            split_axis=0,
+            concat_axis=0,
+        ),
+        dim_no,
+    )
+
+
+_lay_tables = functools.partial(remake_slices_all, mesh_name="band", dim_no=1)
 
 
 def coupling_block(coupling, offsets, counts):
@@ -42,7 +58,7 @@
 
 def shards(waves, projectors, coupling, offsets, counts):
     block = coupling_block(coupling, offsets, counts)
-    gathered = lax.all_gather(projectors, "band", axis=1, tiled=True)
+    gathered = _lay_tables(projectors)
     partial_coeffs = project(gathered, waves)
     coeffs = lax.psum(partial_coeffs, "pw")
     coupled = jnp.einsum("pq,kqb->kpb", block, coeffs, precision=lax.Precision.HIGHEST).astype(

time: 365 us -> 336 us (0.921)
  blocking collectives: 54.1 us -> 30.2 us
  waiting for transfers between devices: 274 us -> 269 us
    all_gather x1 -> x0, blocking collectives: 54.1 us -> none  [shards(): gathered = lax.all_gather(projectors, 'band', axis=1, tiled=True)]
    all_to_all x0 -> x1, blocking collectives: none -> 30.2 us  [remake_slices_all(): jax.lax.all_to_all(jnp.stack([vals] * jax.lax.axis_size(mesh_name), axis=...]
    psum x1, waiting for transfers between devices: 274 us -> 269 us  [shards(): coeffs = lax.psum(partial_coeffs, 'pw')]
where the time goes in v2:
time: 336 us
  waiting for transfers between devices  269 us (80%)
  blocking collectives  30.2 us (9%)
  between operations  13.5 us (4%)
  matrix products  11.1 us (3%)
  local copies, waits for them, and re-layouts  8.58 us (3%)
  other arithmetic  3.6 us (1%)
    psum x1, waiting for transfers between devices, shards(): coeffs = lax.psum(partial_coeffs, 'pw')  269 us
    all_to_all x1, blocking collectives, remake_slices_all(): jax.lax.all_to_all(jnp.stack([vals] * jax.lax.axis_size(mesh_name), axis=...  30.2 us
    another operation x1, local copies, waits for them, and re-layouts, spread_back(): return jnp.stack([real, imag])  7.27 us
  transfers between devices with their start and end apart: 1, of which 1 were waited for; matrix products, arithmetic and copies ran while one was open for 1% of the time, Pallas kernels for 0%

profile of v2, /device:TPU:2, one launch (start us, length us, event | category | flops | bytes accessed | tf_op | source)
XLA Modules:
  0.0 336.0 jit_solution(3935263034095764991)
XLA Ops:
  6.5 0.0 all-reduce.2.cloned.1.call-start
  6.5 0.0 copy-start
  6.5 1.1 stack.32
  7.6 30.2 %all_to_all.5 = bf16[8,2,16,1280]{3,2,1,0:T(8,128)(2,1)S(1)} all-to-all(bf16[8,2,16,1280]{3,2,1,0:T(8,128)(2,1)S(1)} %stack.32), channel_id=1, replica_groups=mesh['pw'=32,'band'=8] {'band'}, dimensions={0} | all-to-all | bytes 1310720 | tf_op jit(solution)/shard_map/all_to_all | solution.py:13
  37.9 2.2 fusion.2
  40.1 0.0 copy-done
  40.1 0.5 fusion.4
  40.6 0.0 copy-start.1
  40.6 0.0 copy-start.2
  40.6 0.0 copy-start.3
  40.6 0.5 fusion.24
  41.2 0.5 fusion.18
  41.7 1.0 pad_maximum_fusion.1
  42.7 0.0 all-reduce.2.cloned.1.call-update
  42.7 0.0 copy-done.1
  42.7 0.2 copy.6
  42.9 0.0 copy-done.2
  42.9 0.1 iota_compare_fusion.1
  42.9 0.0 copy-done.3
  42.9 0.1 iota_add_fusion
  43.0 0.8 fusion.30
  43.8 0.8 fusion.28
  44.6 269.0 %all-reduce.2.cloned.1.call-done = f32[2,128,896]{2,1,0:T(8,128)} async-done(((f32[2,128,896]{2,1,0:T(8,128)}), f32[2,128,896]{2,1,0:T(8,128)}) %all-reduce.2.cloned.1.call-update) | async-done | bytes 917520 | tf_op jit(solution)/shard_map/psum | solution.py:63
  313.6 2.8 fusion.14
  316.4 0.7 fusion.37
  317.2 0.7 fusion.36
  317.9 0.8 fusion.1
  318.7 0.8 fusion
  319.4 2.5 pad_maximum_fusion
  321.9 7.3 %copy.8 = bf16[2,1280,896]{2,1,0:T(8,128)(2,1)} copy(bf16[2,1280,896]{1,2,0:T(8,128)(2,1)} %pad_maximum_fusion) | data formatting | bytes 9175040 | tf_op jit(solution)/shard_map/stack | solution.py:56
  (1 shorter events, 0.0 us)
Async XLA Ops:
  6.5 307.1 %all-reduce.2.cloned.1.call-start = ((), (), s32[]{:S(2)}) async-start(), calls=%async_computation.1 | async-start | bytes 1835008 | tf_op jit(solution)/shard_map/psum | solution.py:63
  6.5 33.5 %copy-start = (bf16[2,1280,896]{2,1,0:T(8,128)(2,1)S(1)}, bf16[2,1280,896]{2,1,0:T(8,128)(2,1)}, u32[]{:S(2)}) copy-start(bf16[2,1280,896]{2,1,0:T(8,128)(2,1)} %param.5) | copy-start | bytes 13762564
  40.6 2.1 copy-start.1
  40.6 2.2 copy-start.2
  40.6 2.3 copy-start.3
Sparse Core Ops, SparseCore 0:
  42.8 270.7 all-reduce.1
